TPU v7x, 128 devices: a whole 4x4x4 slice. The times are simulated.
128 devices in a mesh: fsdp: 64 (over x_lo, y, z, core), rep: 2 (over x_hi).
Axes of the slice: x: 4 (x_hi: 2, x_lo: 2; x = x_hi * 2 + x_lo), y: 4, z: 4, core: 2. Of those that a mesh axis runs over, the one named last changes fastest.
Arguments:
- tokens: bfloat16 [16384, 1024], P(('fsdp', 'rep')), may hold values from -6 to 6
- segment_ids: int32 [256, 64], P(('fsdp', 'rep')), may hold values from 0 to 2, never falling along the last dimension, each value on 1 to 32 neighbouring positions
- routes: int32 [16384, 2], P(('fsdp', 'rep')), may hold values from 0 to 3, all different within a row; in each aligned block of 64 rows (0 to 63, 64 to 127, ...) at most 48 rows name the same one
- gain_attn: bfloat16 [1024], P('fsdp'), may hold values from 0.5 to 1.5
- attn_in: bfloat16 [1024, 2048], P('fsdp'), may hold values from -0.1875 to 0.1875
- attn_out: bfloat16 [1024, 1024], P('fsdp'), may hold values from -0.75 to 0.75
- gain_ffn: bfloat16 [1024], P('fsdp'), may hold values from 0.5 to 1.5
- router: bfloat16 [1024, 4], P('fsdp'), may hold values from -0.09375 to 0.09375
- expert_weight: bfloat16 [4096, 1536], P('fsdp'), may hold values from -0.375 to 0.375
- cotangent: bfloat16 [16384, 1024], P(('fsdp', 'rep')), may hold values from -6 to 6
Outputs:
- output: bfloat16 [16384, 1024], P(('fsdp', 'rep'))
- tokens_grad: float32 [16384, 1024], P(('fsdp', 'rep'))
- gain_attn_grad: float32 [1024], P('fsdp')
- attn_in_grad: float32 [1024, 2048], P('fsdp')
- attn_out_grad: float32 [1024, 1024], P('fsdp')
- gain_ffn_grad: float32 [1024], P('fsdp')
- router_grad: float32 [1024, 4], P('fsdp')
- expert_grad: float32 [4096, 1536], P('fsdp')
Inputs may be any that keep to these rules, and one draw needn't show every extreme that they name: `segment_ids`: within each row the ids never fall and each sequence holds 1 to 32 tokens, one exactly 32. `routes`: each token names 2 different experts; within each aligned block of 64 rows (one micro-batch) no expert is named by more than 48 rows, and 48 is reached in some block.
All inputs are finite; a program needn't handle non-finite values.
Results may differ from a plain program's by a relative error of at most 0.015.
Values may be sent and summed in bfloat16 or wider, within the bound.
A program may use at most 192 MiB of HBM per device.

v0:
```python
import jax
import jax.numpy as jnp
from jax import lax
from jax.sharding import PartitionSpec as P

HEADS = 16
KV_HEADS = 8
HEAD_DIM = 64
FF = 512
EXPERTS = 4
TOP = 2
CAP = 48


EPS = 1e-06


def rope_tables(seg):
    count = seg.shape[0]
    index = jnp.arange(count)
    same = seg[:, None] == seg[None, :]
    before = index[None, :] < index[:, None]
    pos = jnp.sum(jnp.where(same & before, 1.0, 0.0), axis=1)
    half = HEAD_DIM // 2
    freq = 10000.0 ** (-(jnp.arange(half) * 2.0 / HEAD_DIM))
    angle = pos[:, None] * freq[None, :]
    allowed = same & (index[None, :] <= index[:, None])
    return (jnp.cos(angle), jnp.sin(angle), allowed)


def rotate(value, cosine, sine, sign):
    half = HEAD_DIM // 2
    first = value[..., :half]
    second = value[..., half:]
    cos_b = cosine[:, None, :]
    sin_b = sine[:, None, :] * sign
    return jnp.concatenate(
        [first * cos_b - second * sin_b, second * cos_b + first * sin_b], axis=-1
    )


def slot_places(route):
    count = route.shape[0]
    onehot = (route[:, :, None] == jnp.arange(EXPERTS)[None, None, :]).astype(jnp.int32)
    flat = onehot.reshape(count * TOP, EXPERTS)
    earlier = jnp.cumsum(flat, axis=0) - flat
    slot = jnp.sum(earlier * flat, axis=1).reshape(count, TOP)
    return (route * CAP + slot, onehot.astype(jnp.float32))


def collect(gain_attn, attn_in, attn_out, gain_ffn, router, expert_weight):
    block = (
        lax.all_gather(gain_attn, "fsdp", axis=0, tiled=True),
        lax.all_gather(attn_in, "fsdp", axis=0, tiled=True),
        lax.all_gather(attn_out, "fsdp", axis=0, tiled=True),
        lax.all_gather(gain_ffn, "fsdp", axis=0, tiled=True),
        lax.all_gather(router, "fsdp", axis=0, tiled=True),
    )
    experts = lax.all_gather(expert_weight, "fsdp", axis=0, tiled=True)
    return (block, experts)


def fenced_collect(weights, after):
    fenced = lax.optimization_barrier((weights, after))
    return collect(*fenced[0])


def micro_forward(x, seg, route, block, experts):
    gain_one, w_in, w_out, gain_two, w_router = block
    count, width = x.shape
    width_q = HEADS * HEAD_DIM
    width_k = KV_HEADS * HEAD_DIM
    group = HEADS // KV_HEADS
    scale = HEAD_DIM ** (-0.5)
    r1 = lax.rsqrt(jnp.mean(x * x, axis=1, keepdims=True) + EPS)
    a1 = (x * r1 * gain_one.astype(jnp.float32)).astype(jnp.bfloat16)
    qkv = jnp.dot(a1, w_in, preferred_element_type=jnp.float32)
    cosine, sine, allowed = rope_tables(seg)
    query = rotate(qkv[:, :width_q].reshape(count, HEADS, HEAD_DIM), cosine, sine, 1.0).astype(
        jnp.bfloat16
    )
    keys = rotate(
        qkv[:, width_q : width_q + width_k].reshape(count, KV_HEADS, HEAD_DIM), cosine, sine, 1.0
    ).astype(jnp.bfloat16)
    values = qkv[:, width_q + width_k :].reshape(count, KV_HEADS, HEAD_DIM).astype(jnp.bfloat16)
    grouped = query.reshape(count, KV_HEADS, group, HEAD_DIM)
    scores = jnp.einsum("tkgd,ukd->kgtu", grouped, keys, preferred_element_type=jnp.float32) * scale
    scores = jnp.where(allowed[None, None], scores, -1000000000.0)
    peak = jnp.max(scores, axis=-1, keepdims=True)
    weights = jnp.exp(scores - peak)
    total = jnp.sum(weights, axis=-1, keepdims=True)
    probs = weights / total
    logsum = peak + jnp.log(total)
    attn = jnp.einsum(
        "kgtu,ukd->tkgd", probs.astype(jnp.bfloat16), values, preferred_element_type=jnp.float32
    )
    attn = attn.reshape(count, width_q).astype(jnp.bfloat16)
    hidden_state = x + jnp.dot(attn, w_out, preferred_element_type=jnp.float32)
    r2 = lax.rsqrt(jnp.mean(hidden_state * hidden_state, axis=1, keepdims=True) + EPS)
    a2 = (hidden_state * r2 * gain_two.astype(jnp.float32)).astype(jnp.bfloat16)
    logits = jnp.dot(a2, w_router, preferred_element_type=jnp.float32)
    lpeak = jnp.max(logits, axis=1, keepdims=True)
    lexp = jnp.exp(logits - lpeak)
    rprobs = lexp / jnp.sum(lexp, axis=1, keepdims=True)
    gates = jnp.take_along_axis(rprobs, route, axis=1)
    place, onehot = slot_places(route)
    match = place[:, :, None] == jnp.arange(EXPERTS * CAP)[None, None, :]
    dispatch = jnp.sum(match.astype(jnp.float32), axis=1).astype(jnp.bfloat16)
    expert_in = jnp.einsum("tr,td->rd", dispatch, a2, preferred_element_type=jnp.float32).astype(
        jnp.bfloat16
    )
    expert_in = expert_in.reshape(EXPERTS, CAP, width)
    blocks = experts.reshape(EXPERTS, width, 3 * FF)
    gate_up = jnp.einsum(
        "ecd,edf->ecf", expert_in, blocks[:, :, : 2 * FF], preferred_element_type=jnp.float32
    )
    gate_part = gate_up[..., :FF]
    hidden = (gate_part / (1.0 + jnp.exp(-gate_part)) * gate_up[..., FF:]).astype(jnp.bfloat16)
    expert_out = jnp.einsum(
        "ecf,edf->ecd", hidden, blocks[:, :, 2 * FF :], preferred_element_type=jnp.float32
    )
    flat_place = place.reshape(-1)
    picked = expert_out.reshape(EXPERTS * CAP, width)[flat_place].reshape(count, TOP, width)
    output = hidden_state + jnp.sum(gates[:, :, None] * picked, axis=1)
    saved = (
        r1,
        a1,
        cosine,
        sine,
        allowed,
        query,
        keys,
        values,
        logsum,
        attn,
        hidden_state,
        r2,
        a2,
        rprobs,
        gates,
        place,
        onehot,
        match,
        expert_in,
        gate_up,
        hidden,
        picked,
    )
    return (output, saved)


def micro_backward(x, dy, saved, block, experts):
    (
        r1,
        a1,
        cosine,
        sine,
        allowed,
        query,
        keys,
        values,
        logsum,
        attn,
        hidden_state,
        r2,
        a2,
        rprobs,
        gates,
        place,
        onehot,
        match,
        expert_in,
        gate_up,
        hidden,
        picked,
    ) = saved
    gain_one, w_in, w_out, gain_two, w_router = block
    high = lax.Precision.HIGHEST
    count, width = x.shape
    width_q = HEADS * HEAD_DIM
    width_k = KV_HEADS * HEAD_DIM
    group = HEADS // KV_HEADS
    scale = HEAD_DIM ** (-0.5)
    blocks = experts.reshape(EXPERTS, width, 3 * FF)
    combine = jnp.sum(match.astype(jnp.float32) * gates[:, :, None], axis=1)
    d_expert_out = jnp.einsum("tr,td->rd", combine, dy, precision=high)
    dye_low = d_expert_out.astype(jnp.bfloat16).reshape(EXPERTS, CAP, width)
    d_gates = jnp.sum(picked * dy[:, None, :], axis=-1)
    d_hidden = jnp.einsum(
        "ecd,edf->ecf", dye_low, blocks[:, :, 2 * FF :], preferred_element_type=jnp.float32
    )
    gate_part = gate_up[..., :FF]
    up_part = gate_up[..., FF:]
    sig = 1.0 / (1.0 + jnp.exp(-gate_part))
    d_gate = d_hidden * up_part * sig * (1.0 + gate_part * (1.0 - sig))
    d_up = d_hidden * gate_part * sig
    dgu_low = jnp.concatenate([d_gate, d_up], axis=-1).astype(jnp.bfloat16)
    d_expert_in = jnp.einsum(
        "ecf,edf->ecd", dgu_low, blocks[:, :, : 2 * FF], preferred_element_type=jnp.float32
    )
    d_a2 = jnp.sum(
        d_expert_in.reshape(EXPERTS * CAP, width)[place.reshape(-1)].reshape(count, TOP, width),
        axis=1,
    )
    d_probs = jnp.sum(d_gates[:, :, None] * onehot, axis=1)
    d_logits = rprobs * (d_probs - jnp.sum(rprobs * d_probs, axis=1, keepdims=True))
    a2_wide = a2.astype(jnp.float32)
    router_wide = w_router.astype(jnp.float32)
    d_router = jnp.einsum("td,te->de", a2_wide, d_logits, precision=high)
    d_a2 = d_a2 + jnp.einsum("te,de->td", d_logits, router_wide, precision=high)
    g2 = gain_two.astype(jnp.float32)
    d_gain_two = jnp.sum(d_a2 * hidden_state * r2, axis=0)
    scaled_two = g2 * d_a2
    d_state = (
        dy
        + r2 * scaled_two
        - hidden_state * r2**3 * jnp.mean(scaled_two * hidden_state, axis=1, keepdims=True)
    )
    branch_low = d_state.astype(jnp.bfloat16)
    d_w_out = jnp.einsum("tq,td->qd", attn, branch_low, preferred_element_type=jnp.float32)
    d_attn = jnp.einsum("td,qd->tq", branch_low, w_out, preferred_element_type=jnp.float32)
    d_attn_low = d_attn.astype(jnp.bfloat16).reshape(count, KV_HEADS, group, HEAD_DIM)
    grouped = query.reshape(count, KV_HEADS, group, HEAD_DIM)
    scores = jnp.einsum("tkgd,ukd->kgtu", grouped, keys, preferred_element_type=jnp.float32) * scale
    scores = jnp.where(allowed[None, None], scores, -1000000000.0)
    probs = jnp.exp(scores - logsum)
    d_probs_attn = jnp.einsum(
        "tkgd,ukd->kgtu", d_attn_low, values, preferred_element_type=jnp.float32
    )
    d_values = jnp.einsum(
        "kgtu,tkgd->ukd", probs.astype(jnp.bfloat16), d_attn_low, preferred_element_type=jnp.float32
    )
    d_scores = probs * (d_probs_attn - jnp.sum(probs * d_probs_attn, axis=-1, keepdims=True))
    ds_low = d_scores.astype(jnp.bfloat16)
    d_query = jnp.einsum("kgtu,ukd->tkgd", ds_low, keys, preferred_element_type=jnp.float32) * scale
    d_keys = (
        jnp.einsum("kgtu,tkgd->ukd", ds_low, grouped, preferred_element_type=jnp.float32) * scale
    )
    d_query = rotate(d_query.reshape(count, HEADS, HEAD_DIM), cosine, sine, -1.0)
    d_keys = rotate(d_keys, cosine, sine, -1.0)
    d_qkv = jnp.concatenate(
        [
            d_query.reshape(count, width_q),
            d_keys.reshape(count, width_k),
            d_values.reshape(count, width_k),
        ],
        axis=1,
    ).astype(jnp.bfloat16)
    d_w_in = jnp.einsum("td,tw->dw", a1, d_qkv, preferred_element_type=jnp.float32)
    d_a1 = jnp.einsum("tw,dw->td", d_qkv, w_in, preferred_element_type=jnp.float32)
    g1 = gain_one.astype(jnp.float32)
    d_gain_one = jnp.sum(d_a1 * x * r1, axis=0)
    scaled_one = g1 * d_a1
    d_x = d_state + r1 * scaled_one - x * r1**3 * jnp.mean(scaled_one * x, axis=1, keepdims=True)
    grads = (d_gain_one, d_w_in, d_w_out, d_gain_two, d_router)
    expert_saved = (expert_in, dgu_low, dye_low, hidden)
    return (d_x, grads, expert_saved)


def local(
    tokens,
    segment_ids,
    routes,
    gain_attn,
    attn_in,
    attn_out,
    gain_ffn,
    router,
    expert_weight,
    cotangent,
):
    micro_count = segment_ids.shape[0]
    rows_tok = tokens.shape[0] // micro_count
    weights_all = (gain_attn, attn_in, attn_out, gain_ffn, router, expert_weight)
    outputs = []
    token_grads = []
    totals = None
    kept = []
    previous = jnp.zeros((), jnp.float32)
    for index in range(micro_count):
        lower = index * rows_tok
        x_part = tokens[lower : lower + rows_tok].astype(jnp.float32)
        dy_part = cotangent[lower : lower + rows_tok].astype(jnp.float32)
        route_part = routes[lower : lower + rows_tok]
        block, experts = fenced_collect(weights_all, previous)
        output, saved = micro_forward(x_part, segment_ids[index], route_part, block, experts)
        back_block, back_experts = (block, experts)
        d_x, grads, expert_saved = micro_backward(x_part, dy_part, saved, back_block, back_experts)
        previous = d_x
        outputs.append(output.astype(jnp.bfloat16))
        token_grads.append(d_x)
        if totals is None:
            totals = grads
        else:
            totals = tuple((total + grad for total, grad in zip(totals, grads)))
        kept.append(expert_saved)
    expert_in_all = jnp.concatenate([item[0] for item in kept], axis=1)
    dgu_all = jnp.concatenate([item[1] for item in kept], axis=1)
    dye_all = jnp.concatenate([item[2] for item in kept], axis=1)
    hidden_all = jnp.concatenate([item[3] for item in kept], axis=1)
    shard_rows = expert_weight.shape[0]
    block_shards = lax.psum_scatter(totals, "fsdp", scatter_dimension=0, tiled=True)
    part_one = jnp.einsum(
        "ecd,ecf->edf", expert_in_all, dgu_all, preferred_element_type=jnp.float32
    )
    part_two = jnp.einsum("ecd,ecf->edf", dye_all, hidden_all, preferred_element_type=jnp.float32)
    expert_shard = lax.psum_scatter(
        jnp.concatenate([part_one, part_two], axis=-1).reshape(
            shard_rows * lax.axis_size("fsdp"), 3 * FF
        ),
        "fsdp",
        scatter_dimension=0,
        tiled=True,
    )
    summed = (
        lax.psum(block_shards[0].astype(jnp.bfloat16), "rep").astype(jnp.float32),
        lax.psum(block_shards[1].astype(jnp.bfloat16), "rep").astype(jnp.float32),
        lax.psum(block_shards[2].astype(jnp.bfloat16), "rep").astype(jnp.float32),
        lax.psum(block_shards[3].astype(jnp.bfloat16), "rep").astype(jnp.float32),
        lax.psum(block_shards[4].astype(jnp.bfloat16), "rep").astype(jnp.float32),
        lax.psum(expert_shard.astype(jnp.bfloat16), "rep").astype(jnp.float32),
    )
    output_all = jnp.concatenate(outputs, axis=0)
    grad_all = jnp.concatenate(token_grads, axis=0)
    return (output_all, grad_all, summed[0], summed[1], summed[2], summed[3], summed[4], summed[5])


def solution(mesh):
    return jax.shard_map(
        local,
        mesh=mesh,
        in_specs=(
            P(("fsdp", "rep"), None),
            P(("fsdp", "rep"), None),
            P(("fsdp", "rep"), None),
            P("fsdp"),
            P("fsdp", None),
            P("fsdp", None),
            P("fsdp"),
            P("fsdp", None),
            P("fsdp", None),
            P(("fsdp", "rep"), None),
        ),
        out_specs=(
            P(("fsdp", "rep"), None),
            P(("fsdp", "rep"), None),
            P("fsdp"),
            P("fsdp", None),
            P("fsdp", None),
            P("fsdp"),
            P("fsdp", None),
            P("fsdp", None),
        ),
        check_vma=False,
    )
```

profile of v0, /device:TPU:2, one launch (start us, length us, event | category | flops | bytes accessed | tf_op | source)
XLA Modules:
  0.0 1993.0 jit_solution(5418353323726615579)
XLA Ops:
  16.0 144.7 %all-reduce.8 = (bf16[1024]{0:T(1024)(128)(2,1)S(1)}, bf16[1024]{0:T(1024)(128)(2,1)S(1)}) all-reduce(bf16[1024]{0:T(1024)(128)(2,1)S(1)} %dynamic-update-slice, bf16[1024]{0:T(1024)(128)(2,1)S(1)} %dynamic-update-slice.1), channel_id=1, replica_groups=mesh['fsdp'=64,'rep'=2] {'fsdp'}, use_global_device_ids=true, to_apply=%add | all-reduce | flops 2048 | bytes 8192
  162.6 76.5 %all-gather = bf16[64,16,4]{1,2,0:T(4,128)(2,1)S(1)} all-gather(bf16[1,16,4]{1,2,0:T(4,128)(2,1)} %bitcast.234), channel_id=1, replica_groups=mesh['fsdp'=64,'rep'=2] {'fsdp'}, dimensions={0}, use_global_device_ids=true | all-gather | bytes 8320 | tf_op jit(solution)/shard_map/all_gather | solution.py:57
  243.1 1.8 slice_convert_fusion.2
  244.9 3.2 fusion.98
  250.2 2.3 multiply_reduce_fusion.11
  253.9 1.7 gather_fusion.4
  257.4 83.1 %all-gather.13.cloned.1.call-done = bf16[4096,1536]{1,0:T(8,128)(2,1)} async-done(((bf16[64,1536]{1,0:T(8,128)(2,1)}), bf16[4096,1536]{1,0:T(8,128)(2,1)}) %all-gather.13.cloned.1.call-update) | async-done | bytes 12582928 | tf_op jit(solution)/shard_map/all_gather | solution.py:59
  340.5 5.0 fusion.6
  345.5 3.8 multiply_convert_fusion.6
  349.3 3.6 fusion.14
  354.9 6.2 fusion.4
  363.2 2.0 multiply_reduce_fusion.5
  366.7 2.3 multiply_reduce_fusion.7
  369.8 2.4 convolution_convert_fusion.7
  372.3 1.6 fusion.24
  380.9 4.6 fusion.65
  391.0 141.8 %all-reduce.7 = (bf16[1024]{0:T(1024)(128)(2,1)S(1)}, bf16[1024]{0:T(1024)(128)(2,1)S(1)}) all-reduce(bf16[1024]{0:T(1024)(128)(2,1)S(1)} %dynamic-update-slice.2, bf16[1024]{0:T(1024)(128)(2,1)S(1)} %dynamic-update-slice.3), channel_id=1, replica_groups=mesh['fsdp'=64,'rep'=2] {'fsdp'}, use_global_device_ids=true, to_apply=%add.2 | all-reduce | flops 2048 | bytes 8192
  532.8 76.2 %all-gather.1 = bf16[64,16,4]{1,2,0:T(4,128)(2,1)S(1)} all-gather(bf16[1,16,4]{1,2,0:T(4,128)(2,1)S(1)} %bitcast.235), channel_id=1, replica_groups=mesh['fsdp'=64,'rep'=2] {'fsdp'}, dimensions={0}, use_global_device_ids=true | all-gather | bytes 8320 | tf_op jit(solution)/shard_map/all_gather | solution.py:57
  609.8 4.6 fusion.83
  614.3 3.1 fusion.95
  619.6 2.3 multiply_reduce_fusion.9
  625.9 88.7 %all-gather.19.cloned.1.call-done = bf16[4096,1536]{1,0:T(8,128)(2,1)} async-done(((bf16[64,1536]{1,0:T(8,128)(2,1)}), bf16[4096,1536]{1,0:T(8,128)(2,1)}) %all-gather.19.cloned.1.call-update) | async-done | bytes 12582928 | tf_op jit(solution)/shard_map/all_gather | solution.py:59
  714.6 5.1 fusion.2
  719.7 4.4 multiply_convert_fusion.3
  724.1 2.6 fusion
  726.8 1.7 gather_fusion.3
  731.2 3.7 fusion.10
  734.9 1.7 gather_fusion.2
  739.1 1.9 multiply_reduce_fusion.6
  741.8 2.3 convolution_convert_fusion.6
  749.5 8.0 convolution_add_fusion
  758.7 2.3 fusion.37
  761.0 2.4 fusion.26
  763.4 11.1 pad_maximum_fusion
  774.5 24.7 %copy.337 = f32[4,1024,1536]{2,1,0:T(8,128)} copy(f32[4,1024,1536]{1,2,0:T(8,128)} %pad_maximum_fusion) | data formatting | bytes 50331648 | tf_op jit(solution)/shard_map/concatenate | solution.py:308
  800.2 2.6 fusion.88
  804.2 4.8 convolution_add_fusion.1
  809.9 3.8 fusion.73
  813.6 240.9 %reduce-scatter.7.cloned.1.call-done = f32[16,2048]{1,0:T(8,128)} async-done(((f32[1024,2048]{1,0:T(8,128)}), f32[16,2048]{1,0:T(8,128)}) %reduce-scatter.7.cloned.1.call-update) | async-done | bytes 131088 | tf_op jit(solution)/shard_map/reduce_scatter | solution.py:302
  1054.5 1.5 convert_element_type.263
  1056.0 324.2 %reduce-scatter.11.cloned.1.call-done = f32[64,1536]{1,0:T(8,128)} async-done(((f32[4096,1536]{1,0:T(8,128)}), f32[64,1536]{1,0:T(8,128)}) %reduce-scatter.11.cloned.1.call-update) | async-done | bytes 393232 | tf_op jit(solution)/shard_map/reduce_scatter | solution.py:307
  1380.3 1.7 convert_element_type.271
  1382.2 141.4 %all-reduce.6 = (bf16[1024]{0:T(1024)(128)(2,1)S(1)}, bf16[1024]{0:T(1024)(128)(2,1)S(1)}) all-reduce(f32[1024]{0:T(1024)S(1)} %add.233, f32[1024]{0:T(1024)S(1)} %add.236), channel_id=2, replica_groups=mesh['fsdp'=64,'rep'=2] {'fsdp'}, use_global_device_ids=true, to_apply=%region_40.42.clone | all-reduce | flops 2048 | bytes 12288
  1524.6 139.1 %reduce-scatter.13.cloned.1.call-done = f32[16,4]{1,0:T(8,128)} async-done(((f32[1024,4]{1,0:T(8,128)}), f32[16,4]{1,0:T(8,128)}) %reduce-scatter.13.cloned.1.call-update) | async-done | bytes 272
  1664.5 288.1 %reduce-scatter.9.cloned.1.call-done = f32[16,1024]{1,0:T(8,128)} async-done(((f32[1024,1024]{1,0:T(8,128)}), f32[16,1024]{1,0:T(8,128)}) %reduce-scatter.9.cloned.1.call-update) | async-done | bytes 65552 | tf_op jit(solution)/shard_map/reduce_scatter | solution.py:302
  1954.2 11.1 all-reduce.9
  1967.6 15.5 all-reduce.13.cloned.1.call-done
  1984.6 1.7 convert_element_type.272
  (379 shorter events, 65.8 us)
Async XLA Ops:
  7.2 237.7 %all-gather.9.cloned.1.call-start = ((), (), s32[]{:S(2)}) async-start(), calls=%async_computation.4 | async-start | bytes 4259840 | tf_op jit(solution)/shard_map/all_gather | solution.py:54
  7.9 242.2 %all-gather.11.cloned.1.call-start = ((), (), s32[]{:S(2)}) async-start(), calls=%async_computation.5 | async-start | bytes 2129920 | tf_op jit(solution)/shard_map/all_gather | solution.py:55
  8.7 331.8 %all-gather.13.cloned.1.call-start = ((), (), s32[]{:S(2)}) async-start(), calls=%async_computation.6 | async-start | bytes 12779520 | tf_op jit(solution)/shard_map/all_gather | solution.py:59
  9.4 604.9 %all-gather.15.cloned.1.call-start = ((), (), s32[]{:S(2)}) async-start(), calls=%async_computation.7 | async-start | bytes 4259840 | tf_op jit(solution)/shard_map/all_gather | solution.py:54
  162.5 86.6 %copy-start.24 = (f32[64,32]{1,0:T(8,128)}, f32[64,32]{1,0:T(8,128)S(1)}, u32[]{:S(2)}) copy-start(f32[64,32]{1,0:T(8,128)S(1)} %copy.275) | copy-start | bytes 24580
  239.2 14.4 copy-start.44
  242.4 6.2 copy-start.60
  255.8 89.7 %copy-start.31 = (f32[64,2]{1,0:T(8,128)}, f32[64,2]{1,0:T(8,128)S(1)}, u32[]{:S(2)}) copy-start(f32[64,2]{1,0:T(8,128)S(1)} %and_select_fusion.1) | copy-start | bytes 1540
  256.9 88.6 %copy-start.6 = (bf16[192,1024]{1,0:T(8,128)(2,1)}, bf16[192,1024]{1,0:T(8,128)(2,1)S(1)}, u32[]{:S(2)}) copy-start(bf16[192,1024]{1,0:T(8,128)(2,1)S(1)} %convolution_convert_fusion.3) | copy-start | bytes 1179652
  257.4 88.0 %copy-start.2 = (bf16[192,1024]{1,0:T(8,128)(2,1)}, bf16[192,1024]{1,0:T(8,128)(2,1)S(1)}, u32[]{:S(2)}) copy-start(bf16[192,1024]{1,0:T(8,128)(2,1)S(1)} %convolution_convert_fusion.2) | copy-start | bytes 1179652
  365.9 10.0 copy-start.49
  366.6 5.7 copy-start.71
  369.0 7.2 copy-start.14
  369.0 7.3 copy-start.16
  376.2 4.7 copy-start.61
  379.2 6.3 copy-start.82
  379.5 8.1 copy-start.62
  380.5 8.2 copy-start.41
  380.5 8.3 copy-start.33
  380.5 8.7 copy-start.40
  380.5 10.0 copy-start.84
  380.5 10.2 copy-start.85
  380.5 152.3 %copy-start.80 = (bf16[16,4]{0,1:T(4,128)(2,1)S(1)}, bf16[16,4]{0,1:T(4,128)(2,1)}, u32[]{:S(2)}) copy-start(bf16[16,4]{0,1:T(4,128)(2,1)} %param.19) | copy-start | bytes 388
  386.4 233.2 %all-gather.17.cloned.1.call-start = ((), (), s32[]{:S(2)}) async-start(), calls=%async_computation.8 | async-start | bytes 2129920 | tf_op jit(solution)/shard_map/all_gather | solution.py:55
  387.0 327.6 %all-gather.19.cloned.1.call-start = ((), (), s32[]{:S(2)}) async-start(), calls=%async_computation.9 | async-start | bytes 12779520 | tf_op jit(solution)/shard_map/all_gather | solution.py:59
  387.6 667.0 %reduce-scatter.7.cloned.1.call-start = ((), (), s32[]{:S(2)}) async-start(), calls=%async_computation.10 | async-start | bytes 8519680 | tf_op jit(solution)/shard_map/reduce_scatter | solution.py:302
  388.9 229.7 %copy-start.32 = (f32[64,32]{1,0:T(8,128)}, f32[64,32]{1,0:T(8,128)S(1)}, u32[]{:S(2)}) copy-start(f32[64,32]{1,0:T(8,128)S(1)} %copy.308) | copy-start | bytes 24580
  532.8 81.5 %copy-start.42 = (f32[1024]{0:T(1024)}, f32[1024]{0:T(1024)S(1)}, u32[]{:S(2)}) copy-start(f32[1024]{0:T(1024)S(1)} %convert_element_type.238) | copy-start | bytes 12292
  532.8 89.7 %copy-start.47 = (f32[1024]{0:T(1024)}, f32[1024]{0:T(1024)S(1)}, u32[]{:S(2)}) copy-start(f32[1024]{0:T(1024)S(1)} %convert_element_type.245) | copy-start | bytes 12292
  609.2 13.4 copy-start.45
  618.7 5.9 copy-start.12
  625.3 94.4 %copy-start.8 = (bf16[192,1024]{1,0:T(8,128)(2,1)}, bf16[192,1024]{1,0:T(8,128)(2,1)S(1)}, u32[]{:S(2)}) copy-start(bf16[192,1024]{1,0:T(8,128)(2,1)S(1)} %convolution_convert_fusion.1) | copy-start | bytes 1179652
  625.8 93.8 %copy-start.4 = (bf16[192,1024]{1,0:T(8,128)(2,1)}, bf16[192,1024]{1,0:T(8,128)(2,1)S(1)}, u32[]{:S(2)}) copy-start(bf16[192,1024]{1,0:T(8,128)(2,1)S(1)} %convolution_convert_fusion) | copy-start | bytes 1179652
  714.6 9.6 copy-start.10
  731.2 6.8 copy-start.19
  734.9 6.1 copy-start.83
  757.6 622.7 %reduce-scatter.11.cloned.1.call-start = ((), (), s32[]{:S(2)}) async-start(), calls=%async_computation.12 | async-start | bytes 25559040 | tf_op jit(solution)/shard_map/reduce_scatter | solution.py:307
  799.3 4.9 copy-start.21
  799.3 864.5 %reduce-scatter.13.cloned.1.call-start = ((), (), s32[]{:S(2)}) async-start(), calls=%async_computation.13 | async-start | bytes 532480
  804.1 1148.6 %reduce-scatter.9.cloned.1.call-start = ((), (), s32[]{:S(2)}) async-start(), calls=%async_computation.11 | async-start | bytes 4259840 | tf_op jit(solution)/shard_map/reduce_scatter | solution.py:302
  809.0 573.0 %copy-start.81 = (f32[64]{0:T(128)S(1)}, f32[64]{0:T(128)}, u32[]{:S(2)}) copy-start(f32[64]{0:T(128)} %get-tuple-element.111) | copy-start | bytes 772
  809.0 573.1 %copy-start.59 = (f32[1024]{0:T(1024)S(1)}, f32[1024]{0:T(1024)}, u32[]{:S(2)}) copy-start(f32[1024]{0:T(1024)} %get-tuple-element.39) | copy-start | bytes 12292
  809.0 573.1 %copy-start.57 = (f32[1024]{0:T(1024)S(1)}, f32[1024]{0:T(1024)}, u32[]{:S(2)}) copy-start(f32[1024]{0:T(1024)} %get-tuple-element.35) | copy-start | bytes 12292
  809.0 573.1 %copy-start.58 = (f32[1024]{0:T(1024)S(1)}, f32[1024]{0:T(1024)}, u32[]{:S(2)}) copy-start(f32[1024]{0:T(1024)} %get-tuple-element.33) | copy-start | bytes 12292
  809.1 714.7 %copy-start.23 = (f32[64,1024]{1,0:T(8,128)S(1)}, f32[64,1024]{1,0:T(8,128)}, u32[]{:S(2)}) copy-start(f32[64,1024]{1,0:T(8,128)} %fusion.62) | copy-start | bytes 786436
  809.1 1144.5 %copy-start.29 = (bf16[64,1024]{1,0:T(8,128)(2,1)S(1)}, bf16[64,1024]{1,0:T(8,128)(2,1)}, u32[]{:S(2)}) copy-start(bf16[64,1024]{1,0:T(8,128)(2,1)} %get-tuple-element.88) | copy-start | bytes 393220
  809.1 1144.4 %copy-start.30 = (bf16[64,1024]{1,0:T(8,128)(2,1)S(1)}, bf16[64,1024]{1,0:T(8,128)(2,1)}, u32[]{:S(2)}) copy-start(bf16[64,1024]{1,0:T(8,128)(2,1)} %get-tuple-element.87) | copy-start | bytes 393220
  809.1 1174.0 %all-reduce.13.cloned.1.call-start = ((), (), s32[]{:S(2)}) async-start(), calls=%async_computation.14 | async-start | bytes 524288 | tf_op jit(solution)/shard_map/psum | solution.py:317
  (49 other events, 130.7 us)
Sparse Core Ops, SparseCore 0:
  9.7 107.7 all-gather.8
  119.2 102.2 all-gather.10
  223.3 117.1 all-gather.12
  386.5 105.1 all-gather.14
  493.3 102.4 all-gather.16
  597.3 117.1 all-gather.18
  757.7 296.8 reduce-scatter.6
  1056.9 323.2 reduce-scatter.10
  1382.6 281.0 reduce-scatter.12
  1666.1 286.5 reduce-scatter.8
  1955.7 27.3 all-reduce.12
where the time goes:
time: 2010 us; the launch traced here: 1990 us
  waiting for transfers between devices  1180 us (59%)
  blocking collectives  592 us (29%)
  matrix products  97.5 us (5%)
  local copies, waits for them, and re-layouts  56.6 us (3%)
  other arithmetic  46.4 us (2%)
    reduce_scatter x2, waiting for transfers between devices, local(): lax.psum_scatter(totals, 'fsdp', scatter_dimension=0, tiled=True)  529 us
    unnamed x3, blocking collectives  428 us
    reduce_scatter x1, waiting for transfers between devices, local(): lax.psum_scatter(jnp.concatenate([part_one, part_two], axis=-1).reshape(s...  324 us
    all_gather x2, waiting for transfers between devices, collect(): experts = lax.all_gather(expert_weight, 'fsdp', axis=0, tiled=True)  172 us
    all_gather x2, blocking collectives, collect(): lax.all_gather(router, 'fsdp', axis=0, tiled=True)  153 us
    unnamed x12, waiting for transfers between devices  142 us
  transfers between devices with their start and end apart: 11, of which 7 were waited for; matrix products, arithmetic and copies ran while one was open for 5% of the time, Pallas kernels for 0%

commit v1 on v0

v1 whole, which is shorter than its diff:
```python
import functools

import jax
import jax.numpy as jnp
from jax import lax
from jax.experimental import pallas as pl
from jax.experimental.pallas import tpu as pltpu
from jax.sharding import PartitionSpec as P

EPS = 1e-06
D = 1024
FF = 512
EXPERTS = 4
TOK = 128
COLS_W = 1536
SHARE = 768
ROWS_A = 16
ROWS_W = 64
MISC = 2048
EXTRA = 1152
HALF = 64
MESH = pl.DeviceIdType.MESH
F32 = jnp.float32
BF16 = jnp.bfloat16
WIDE = {"x": 2, "y": 4, "z": 4}

GATHERS = (
    (0, 0, 1024, "xyz"),
    (0, 1024, 1152, "xzy"),
    (1, 0, 512, "yzx"),
    (1, 512, 512, "zyx"),
    (2, 0, 384, "yz"),
    (2, 384, 384, "zy"),
)
SUMS = (
    (0, 0, 512, "xyz"),
    (0, 512, 512, "xzy"),
    (0, 1024, 512, "xyz"),
    (0, 1536, 512, "xzy"),
    (1, 0, 512, "yzx"),
    (1, 512, 640, "zyx"),
    (2, 0, 384, "yz"),
    (2, 384, 384, "zy"),
)
TILES = (0, 1, 4, 6, 2, 3, 5, 7)
INPUTS, OUTPUTS, EXPERTS_IN = (0, 1), (2, 3), (4, 5)
EARLY, LATE, OUT_SUMS, EXPERT_SUMS = (0, 1), (2, 3), (4, 5), (6, 7)
SUM_ORDER = EXPERT_SUMS + OUT_SUMS + EARLY + LATE
ROWS = (ROWS_A, ROWS_A, 2 * ROWS_W)


def unit_shape(unit):
    cores = (2,) if unit[0] < 2 else ()
    return cores + tuple(WIDE[axis] for axis in reversed(unit[3])) + (ROWS[unit[0]], unit[2])


def place():
    fsdp = lax.axis_index("fsdp")
    rep = lax.axis_index("rep")
    core = lax.rem(fsdp, 2)
    z = lax.rem(fsdp // 2, 4)
    y = lax.rem(fsdp // 8, 4)
    xl = fsdp // 32
    return {"x": xl, "y": y, "z": z, "c": core, "r": rep}


def device(at):
    return (at["x"] * 32 + at["y"] * 8 + at["z"] * 2 + at["c"], at["r"])


def shifted(at, axis, step):
    new = dict(at)
    if axis == "x":
        whole = lax.rem(at["r"] * 2 + at["x"] + step + 4, 4)
        new["x"] = lax.rem(whole, 2)
        new["r"] = whole // 2
    elif axis == "c":
        new["c"] = 1 - at["c"]
    else:
        new[axis] = lax.rem(at[axis] + step + 4, 4)
    return new


def greet(devices):
    barrier = pltpu.get_barrier_semaphore()
    for other in devices:
        pl.semaphore_signal(barrier, inc=1, device_id=device(other), device_id_type=MESH)


def meet(devices):
    pl.semaphore_wait(pltpu.get_barrier_semaphore(), len(devices))


ALL = slice(None)


class Piece:
    def __init__(self, order, spots, columns=ALL, rows=ALL):
        self.order, self.spots, self.columns, self.rows = order, spots, columns, rows

    def moved(self, axis, spot):
        return Piece(self.order, {**self.spots, axis: spot}, self.columns, self.rows)

    def full(self, axis):
        return self.moved(axis, (0, WIDE[axis]))

    def index(self, core, spots=None):
        spots = spots or self.spots
        lead = [spots[axis] for axis in reversed(self.order)]
        lead = [pl.ds(*spot) if isinstance(spot, tuple) else spot for spot in lead]
        return (*(() if core is None else (core,)), *lead, self.rows, self.columns)

    def of(self, ref, core):
        return ref.at[self.index(core)]

    def halves(self, rows, count):
        for axis in reversed(self.order):
            if isinstance(self.spots[axis], tuple):
                middle = WIDE[axis] // 2
                return [self.moved(axis, (0, middle)), self.moved(axis, (middle, middle))]
        first = count // 256 * 128
        return [Piece(self.order, self.spots, pl.ds(*run), ALL) for run in ((0, first), (first, count - first))]

    def shape(self, rows, count):
        lead = [self.spots[axis] for axis in reversed(self.order)]
        lead = tuple(spot[1] for spot in lead if isinstance(spot, tuple))
        size = [whole if part == ALL else part.size for part, whole in ((self.rows, rows), (self.columns, count))]
        return lead + tuple(size)


class Links:
    def __init__(self, at, send, recv, free, partners):
        self.at, self.send, self.recv, self.free, self.partners = at, send, recv, free, partners
        self.used, self.open = 0, []

    def turn(self):
        self.close()
        self.used, self.open = 0, []
        for other in self.partners:
            pl.semaphore_signal(self.free, inc=1, device_id=device(other), device_id_type=MESH)

    def turned(self):
        pl.semaphore_wait(self.free, len(self.partners))

    def local(self, source, target):
        copy = pltpu.make_async_copy(source, target, self.send.at[self.used])
        self.used += 1
        copy.start()
        return copy

    def push(self, source, target, to):
        copy = pltpu.make_async_remote_copy(
            src_ref=source,
            dst_ref=target,
            send_sem=self.send.at[self.used],
            recv_sem=self.recv.at[self.used],
            device_id=device(to),
            device_id_type=MESH,
        )
        self.used += 1
        copy.start()
        self.open.append(copy)
        return copy

    def close(self):
        for copy in self.open:
            copy.wait_send()


class Gather:
    def __init__(self, links, src, dst, unit):
        self.links, self.at, self.src, self.dst = links, links.at, src, dst
        array, self.first, self.count, self.order = unit
        self.rows = ROWS[array]
        self.core = self.at["c"] if array < 2 else None
        self.handed = []

    def push(self, source, piece, target):
        spot = piece.of(self.dst, self.core)
        return self.links.push(spot if source is None else source, spot, target)

    def sibling(self, piece, source=None):
        if self.core is None:
            return
        self.handed.append(self.push(source, piece, shifted(self.at, "c", 0)))

    def source_of(self, piece):
        columns = piece.columns
        if columns == ALL:
            columns = pl.ds(self.first, self.count)
        else:
            columns = pl.ds(self.first + columns.start, columns.size)
        return self.src.at[:, columns]

    def steps(self):
        at, order = self.at, self.order
        have = Piece(order, {axis: at[axis] for axis in order})
        if self.core is None:
            rows = pl.ds(pl.multiple_of(ROWS_W * at["c"], ROWS_W), ROWS_W)
            block = Piece(order, have.spots, ALL, rows)
            own, theirs = (src.at[:, pl.ds(self.first, self.count)] for src in self.src)
            local = self.links.local(own, block.of(self.dst, None))
            copy = self.push(theirs, block, shifted(at, "c", 0))
            yield
            local.wait()
            copy.wait_recv()
            mine = None
        else:
            mine = self.source_of(have)
            local = self.links.local(mine, have.of(self.dst, self.core))
        plane = order[:2] if order[0] == "x" else order[:1]
        ring = plane[-1]
        direct = [self.push(mine, have, shifted(at, ring, step)) for step in (1, -1, 2)]
        if "x" in plane:
            halves = have.halves(self.rows, self.count)
            for step in (0, 1, -1, 2):
                for half, side in zip(halves, (1, -1)):
                    target = shifted(shifted(at, "x", side), ring, step)
                    direct.append(self.push(self.source_of(half), half, target))
        yield
        if self.core is not None:
            local.wait()
        for copy in direct:
            copy.wait_recv()
        for axis in plane:
            have = have.full(axis)
        for axis in order[len(plane) :]:
            if axis == "x":
                halves = have.halves(self.rows, self.count)
                moved = [self.push(None, half, shifted(at, "x", side)) for half, side in zip(halves, (1, -1))]
                yield
                for copy in moved:
                    copy.wait_recv()
                self.sibling(have.moved("x", 1 - at["x"]))
                return
            near = [self.push(None, have, shifted(at, axis, step)) for step in (1, -1)]
            self.sibling(have)
            yield
            fresh = [have.moved(axis, shifted(at, axis, -step)[axis]) for step in (1, -1)]
            far = []
            for index, step in enumerate((1, -1)):
                near[index].wait_recv()
                piece = fresh[index].halves(self.rows, self.count)[index]
                far.append(self.push(None, piece, shifted(at, axis, step)))
            for piece in fresh:
                self.sibling(piece)
            yield
            for copy in far:
                copy.wait_recv()
            self.sibling(have.moved(axis, shifted(at, axis, 2)[axis]))
            have = have.full(axis)

    def settle(self):
        for copy in self.handed:
            copy.wait_recv()


class Group:
    def __init__(self, flows):
        self.flows = flows
        self.live = [flow.steps() for flow in flows]

    def step(self, times=1):
        for unused in range(times):
            self.live = [flow for flow in self.live if next(flow, "end") != "end"]

    def run(self):
        while self.live:
            self.step()

    def settle(self):
        self.run()
        for flow in self.flows:
            flow.settle()


def add_blocks(ref, piece, core, others):
    runs = [axis for axis in reversed(piece.order) if isinstance(piece.spots[axis], tuple)]
    loops = runs[:-1]
    total = 1
    for axis in loops:
        total *= piece.spots[axis][1]

    def step(i, carry):
        left, spots = i, dict(piece.spots)
        index = []
        for axis in reversed(loops):
            start, length = piece.spots[axis]
            spot = lax.rem(left, length)
            index.insert(0, spot)
            spots[axis] = start + spot
            left = left // length
        where = piece.index(core, spots)
        terms = [ref[where]]
        terms += [other[tuple(index) + (ALL,) * (len(other.shape) - len(index))] for other in others]
        if len(terms) > 2:
            terms = [term.astype(F32) for term in terms]
        ref[where] = functools.reduce(jnp.add, terms).astype(BF16)
        return carry

    if loops:
        lax.fori_loop(0, total, step, 0)
    else:
        step(0, 0)


class Scatter:
    def __init__(self, links, grad, out, unit, buffers):
        self.links, self.at, self.grad, self.out = links, links.at, grad, out
        array, self.first, self.count, self.order = unit
        self.unit, self.rows = unit, ROWS[array]
        self.buffers = list(buffers)

    @staticmethod
    def shapes(unit):
        rows, count, order = ROWS[unit[0]], unit[2], unit[3]
        piece = Piece(order, {axis: (0, WIDE[axis]) for axis in order})
        shapes = [piece.shape(rows, count)] if unit[0] < 2 else []
        rest = list(reversed(order))
        if order[-1] == "x":
            piece = piece.moved("x", 0)
            shapes += [half.shape(rows, count) for half in piece.halves(rows, count)]
            rest.pop(0)
        piece = piece.moved(rest[0], 0)
        shapes += [half.shape(rows, count) for half in piece.halves(rows, count)]
        shapes += [piece.shape(rows, count)] * 2
        shapes += [piece.moved(rest[1], 0).shape(rows, count)] * 3
        return shapes + [(rows, count)] * (3 if order[0] == "x" else 1)

    def push(self, piece, core, target):
        buffer = self.buffers.pop(0)
        return self.links.push(piece.of(self.grad, core), buffer, target), buffer

    def steps(self):
        at, rows, count = self.at, self.rows, self.count
        core = at["c"] if self.unit[0] < 2 else None
        piece = Piece(self.order, {axis: (0, WIDE[axis]) for axis in self.order})
        last = self.order[-1]
        if core is not None:
            copy, buffer = self.push(piece, 1 - core, shifted(at, "c", 0))
            yield
            copy.wait_recv()
            add_blocks(self.grad, piece, core, [buffer])
        rest = list(reversed(self.order))
        if last == "x":
            theirs = piece.moved("x", 1 - at["x"]).halves(rows, count)
            moved = [self.push(half, core, shifted(at, "x", step)) for half, step in zip(theirs, (1, -1))]
            yield
            piece = piece.moved("x", at["x"])
            for (copy, buffer), half in zip(moved, piece.halves(rows, count)):
                copy.wait_recv()
                add_blocks(self.grad, half, core, [buffer])
            rest.pop(0)
        last, ring = rest[:2]
        theirs = piece.moved(last, shifted(at, last, 2)[last]).halves(rows, count)
        far = [self.push(half, core, shifted(at, last, step)) for half, step in zip(theirs, (1, -1))]
        yield
        near = []
        for index, step in enumerate((1, -1)):
            theirs = piece.moved(last, shifted(at, last, step)[last])
            copy, buffer = far[index]
            copy.wait_recv()
            add_blocks(self.grad, theirs.halves(rows, count)[index], core, [buffer])
            near.append(self.push(theirs, core, shifted(at, last, step)))
        yield
        piece = piece.moved(last, at[last])
        for copy, buffer in near:
            copy.wait_recv()
        add_blocks(self.grad, piece, core, [buffer for copy, buffer in near])
        moves = [shifted(at, ring, step) for step in (1, -1, 2)]
        direct = [self.push(piece.moved(ring, to[ring]), core, to) for to in moves]
        yield
        piece = piece.moved(ring, at[ring])
        for copy, buffer in direct:
            copy.wait_recv()
        add_blocks(self.grad, piece, core, [buffer for copy, buffer in direct])
        if self.order[0] == "x":
            other = piece.moved("x", 1 - at["x"])
            piece = piece.moved("x", at["x"])
            ends = [self.push(piece, core, shifted(at, "x", 2))]
            ends += [self.push(other, core, shifted(at, "x", side)) for side in (1, -1)]
        else:
            ends = [self.push(piece, core, shifted(at, "x", 2))]
        yield
        for copy, buffer in ends:
            copy.wait_recv()
        total = self.grad[piece.index(core)].astype(F32) + ends[0][1][...].astype(F32)
        if len(ends) > 1:
            total = total + (ends[1][1][...].astype(F32) + ends[2][1][...].astype(F32))
        if core is not None:
            self.out[:, pl.ds(self.first, count)] = total
            return
        sums, shared, arriving = self.out
        lower = pl.multiple_of(ROWS_W * at["c"], ROWS_W)
        columns = pl.ds(self.first, count)
        shared[:, columns] = total
        theirs = shared.at[pl.ds(ROWS_W - lower, ROWS_W), columns]
        copy = self.links.push(theirs, arriving.at[:, columns], shifted(at, "c", 0))
        yield
        copy.wait_recv()
        for tile in range(self.first // 128, (self.first + count) // 128):
            local = pl.ds(128 * tile, 128)
            base = FF * (tile // 2) + 128 * (tile % 2)
            mine = pl.ds(pl.multiple_of(base + 256 * at["c"], 128), 128)
            other = pl.ds(pl.multiple_of(base + 256 * (1 - at["c"]), 128), 128)
            sums[:, mine] = shared[pl.ds(lower, ROWS_W), local]
            sums[:, other] = arriving[:, local]

    def settle(self):
        pass


def mm(a, b):
    return jnp.dot(a, b, preferred_element_type=F32)


def mm_nt(a, b):
    return lax.dot_general(a, b, (((1,), (1,)), ((), ())), preferred_element_type=F32)


def mm_tn(a, b):
    return lax.dot_general(a, b, (((0,), (0,)), ((), ())), preferred_element_type=F32)


def turn(value, cosine, sine):
    width = value.shape[1]
    lane = lax.broadcasted_iota(jnp.int32, (1, width), 1)
    low = lax.rem(lane, 64) < 32
    swapped = jnp.where(low, pltpu.roll(value, width - 32, 1), pltpu.roll(value, 32, 1))
    return value * cosine + swapped * sine


def doubled(block, odd, low):
    other = pltpu.roll(block.astype(F32), 64, 1).astype(BF16)
    return jnp.where(low, other, block) if odd else jnp.where(low, block, other)


def split_two(value):
    top = value.astype(BF16)
    return top, (value - top.astype(F32)).astype(BF16)


LAYER_SCRATCH = (
    pltpu.VMEM((ROWS_A, MISC + 128), BF16),
    pltpu.VMEM((ROWS_A, MISC), F32),
    pltpu.VMEM((ROWS_A, D + 128), F32),
    pltpu.VMEM((ROWS_W, SHARE), BF16),
    pltpu.VMEM((ROWS_W, SHARE), BF16),
    pltpu.VMEM((2 * ROWS_W, SHARE), F32),
    pltpu.VMEM((ROWS_W, SHARE), F32),
    pltpu.VMEM((TOK, 2048), BF16),
    pltpu.VMEM((TOK, D), BF16),
    pltpu.VMEM((8, 2 * TOK, TOK), F32),
    pltpu.VMEM((TOK, 2048), BF16),
    pltpu.VMEM((TOK, D), BF16),
    pltpu.VMEM((TOK, D), BF16),
    pltpu.VMEM((TOK, D), F32),
    pltpu.VMEM((TOK, D), F32),
    pltpu.VMEM((TOK, D), F32),
    pltpu.VMEM((D, TOK), BF16),
    pltpu.VMEM((D, TOK), BF16),
    pltpu.VMEM((4 * TOK, EXTRA), BF16),
    pltpu.VMEM((4 * TOK, D), BF16),
    pltpu.VMEM((2, 4 * TOK, SHARE), BF16),
    pltpu.VMEM((2 * TOK, D), F32),
    pltpu.VMEM((2 * TOK, D), F32),
    pltpu.VMEM((4 * TOK, 128), F32),
    pltpu.VMEM((2 * TOK, EXTRA), BF16),
    pltpu.VMEM((2 * TOK, EXTRA), BF16),
    pltpu.VMEM((TOK, EXTRA), BF16),
    pltpu.VMEM((TOK, EXTRA), BF16),
    pltpu.VMEM((2 * TOK, D), BF16),
    pltpu.VMEM((2 * TOK, D), BF16),
    pltpu.VMEM((TOK, D), BF16),
    pltpu.VMEM((TOK, D), BF16),
    pltpu.VMEM((D, 4 * TOK), BF16),
    pltpu.VMEM((D, 4 * TOK), BF16),
)


def whole_body(
    x_ref, g_ref, seg_ref, route_ref, in_ref, aout_ref, gain1_ref, gain2_ref, router_ref, expert_ref,
    out_ref, dx_ref, sum_in, sum_out, small_ref, sum_w,
    src_in, sum_all, sum_more, src_own, src_peer, shared, arriving, qkv, attn, probs, dqkv, a1_ref, dattn_ref, h_ref, dh_ref, da1_ref, a1t, attnt,
    a2_all, g_all, mid, da2_ref, y_ref, dg_ref, sib_d, from_d, ret_d, got_d, sib_y, from_y, ret_y, got_y, a2t, gt, *rest,
):
    at = place()
    ahead, behind = shifted(at, "x", 1), shifted(at, "x", -1)

    around = [shifted(at, axis, step) for axis in "yz" for step in (1, -1, 2)]
    around += [shifted(shifted(at, "x", side), axis, step) for axis in "yz" for step in (1, -1, 2) for side in (1, -1)]
    around += [shifted(at, "x", step) for step in (1, -1, 2)]
    around += [shifted(at, "c", 0)]
    links = Links(at, *rest[-5:-2], around)
    pairs = Links(at, *rest[-2:], None, None)
    greet(around)

    eight = lax.broadcasted_iota(jnp.int32, (8, 128), 0)
    eye = jnp.where(eight == lax.broadcasted_iota(jnp.int32, (8, 128), 1), 1.0, 0.0)
    small = [ref[...].astype(F32) for ref in (router_ref, gain1_ref, gain2_ref)]
    small = jnp.concatenate(small + [jnp.zeros((2, ROWS_A), F32)], axis=0)
    src_in[:, pl.ds(MISC, 128)] = mm_tn(small.astype(BF16), eye.astype(BF16)).astype(BF16)
    for slot, tile in enumerate(TILES):
        src_in[:, pl.ds(256 * slot, 256)] = in_ref[:, pl.ds(256 * tile, 256)]

    for index in range(3):
        target = pl.ds(256 * index, 256)
        for half, columns in ((at["c"], src_own), (1 - at["c"], src_peer)):
            columns[:, target] = expert_ref[:, pl.ds(pl.multiple_of(FF * index + 256 * half, 256), 256)]

    meet(around)

    sources = (src_in, aout_ref, (src_own, src_peer))
    sums = (sum_all, sum_more, (sum_w, shared, arriving))
    buffers = list(rest[:-5])

    weights, grads = buffers[: len(GATHERS)], buffers[len(GATHERS) : len(GATHERS) + len(SUMS)]
    del buffers[: len(GATHERS) + len(SUMS)]

    def gathers(units):
        return Group([Gather(links, sources[GATHERS[u][0]], weights[u], GATHERS[u]) for u in units])

    def scatters(*units):
        flows = []
        for u in units:
            number = len(Scatter.shapes(SUMS[u]))
            mine = buffers[:number]
            del buffers[:number]
            flows.append(Scatter(links, grads[u], sums[SUMS[u][0]], SUMS[u], mine))
        return Group(flows)

    def swap(source, target, first_source, first_target):
        rows = ((0, ahead), (HALF, behind))
        return [
            pairs.push(
                source.at[pl.ds(first_source + lower, HALF)], target.at[pl.ds(first_target + lower, HALF)], to
            )
            for lower, to in rows
        ]

    def swap_back(source, target):
        rows = ((0, behind), (HALF, ahead))
        return [
            pairs.push(source.at[pl.ds(lower, HALF)], target.at[pl.ds(lower, HALF)], to) for lower, to in rows
        ]

    def arrived(copies):
        for copy in copies:
            copy.wait_recv()

    def spot(unit, **where):
        return tuple(where[axis] for axis in ("c",) + tuple(reversed(unit[3])))

    def blocks_a(xs=(0, 1), ys=(0, 1, 2, 3)):
        return [dict(x=x, y=y, z=z, c=c) for x in xs for y in ys for z in range(4) for c in range(2)]

    def cols_a(u, lower, count, **some):
        return jnp.concatenate(
            [weights[u][spot(GATHERS[u], **where) + (ALL, pl.ds(lower, count))] for where in blocks_a(**some)],
            axis=0,
        )

    def tile_a(u, t, count, lower=0):
        return cols_a(u, lower, count, xs=(t // 2,), ys=(2 * (t % 2), 2 * (t % 2) + 1))

    def put_a(u, lower, value):
        value, count = value.astype(BF16), value.shape[1]
        for i, where in enumerate(blocks_a()):
            grads[u][spot(SUMS[u], **where) + (ALL, pl.ds(lower, count))] = value[ROWS_A * i : ROWS_A * (i + 1)]

    def blocks_w(el, ys=(0, 1), zs=(0, 1, 2, 3)):
        return [dict(y=2 * el + y, z=z) for y in ys for z in zs]

    def spot_w(unit, y, z):
        return (z, y) if unit[3] == "yz" else (y, z)

    def cols_w(el, lower, count, **some):
        runs = []
        for u, start in zip(EXPERTS_IN, (0, 384)):
            low_col, high_col = max(lower, start), min(lower + count, start + 384)
            if low_col < high_col:
                columns = pl.ds(low_col - start, high_col - low_col)
                blocks = [weights[u][spot_w(GATHERS[u], **at_w) + (ALL, columns)] for at_w in blocks_w(el, **some)]
                runs.append(jnp.concatenate(blocks, axis=0))
        return runs[0] if len(runs) == 1 else jnp.concatenate(runs, axis=1)

    def put_w(el, lower, value):
        value, count = value.astype(BF16), value.shape[1]
        for u, start in zip(EXPERT_SUMS, (0, 384)):
            low_col, high_col = max(lower, start), min(lower + count, start + 384)
            if low_col < high_col:
                columns = pl.ds(low_col - start, high_col - low_col)
                for i, at_w in enumerate(blocks_w(el)):
                    block = value[128 * i : 128 * (i + 1), low_col - lower : high_col - lower]
                    grads[u][spot_w(SUMS[u], **at_w) + (ALL, columns)] = block

    inputs, outputs, experts = gathers(INPUTS), gathers(OUTPUTS), gathers(EXPERTS_IN)
    inputs.step()
    experts.step()

    own = pl.ds(0, TOK)
    g_all[own, :] = g_ref[...]
    x = x_ref[...].astype(F32)
    r1 = lax.rsqrt(jnp.mean(x * x, axis=1, keepdims=True) + EPS)
    ids = jnp.concatenate([seg_ref[0:1, :], seg_ref[1:2, :] + 4], axis=1).astype(F32)
    rows = jnp.concatenate([ids, route_ref[...].astype(F32), jnp.zeros((TOK - 3, TOK), F32)], axis=0)
    columns = rows.T
    lane = lax.broadcasted_iota(jnp.int32, (1, 128), 1)
    low = lane < 64
    same = columns[:, 0:1] == ids
    t_index = lax.broadcasted_iota(jnp.int32, (TOK, TOK), 0)
    u_index = lax.broadcasted_iota(jnp.int32, (TOK, TOK), 1)
    pos = jnp.sum(jnp.where(same & (u_index < t_index), 1.0, 0.0), axis=1, keepdims=True)
    allowed = same & (u_index <= t_index)
    allowed2 = jnp.concatenate([allowed, allowed], axis=0)
    route0, route1 = columns[:, 1:2].astype(jnp.int32), columns[:, 2:3].astype(jnp.int32)
    named = (route0 == lane) | (route1 == lane)
    inputs.step()
    outputs.step()
    power = lax.rem(lane, 32).astype(F32) * (2.0 / 64)
    angle = pos * jnp.exp(power * (-9.210340371976184))
    cosine = jnp.cos(angle)
    sine = jnp.where(lax.rem(lane, 64) < 32, -1.0, 1.0) * jnp.sin(angle)
    cos4 = jnp.concatenate([cosine] * 2, axis=1)
    sin4 = jnp.concatenate([sine] * 2, axis=1)
    inputs.step()
    outputs.step()
    experts.step()
    inputs.run()
    outputs.step()
    experts.step()
    inputs.settle()

    misc = cols_a(1, 1024, 128)
    row = lax.broadcasted_iota(jnp.int32, (16, 128), 0)
    lane16 = lax.broadcasted_iota(jnp.int32, (16, 128), 1)
    gains = mm_nt(jnp.where(lane16 == row + 4, 1.0, 0.0).astype(BF16), misc)
    gain1, gain2 = gains[0:1], gains[1:2]
    a1_ref[...] = (x * r1 * gain1).astype(BF16)
    for j in range(8):
        block = mm(a1_ref[...], cols_a(j // 4, 256 * (j % 4), 256))
        if TILES[j] < 6:
            block = turn(block, cos4, sin4)
        qkv[:, pl.ds(256 * TILES[j], 256)] = block.astype(BF16)
        if j == 0:
            g_copies = swap(g_ref, g_all, 0, TOK)
            g_own = pairs.push(g_ref, g_all.at[pl.ds(2 * TOK, TOK)], shifted(at, "c", 0))
    outputs.step()

    def heads(ref, k):
        pair = ref[:, pl.ds(128 * k, 128)]
        zero = jnp.zeros_like(pair)
        return jnp.concatenate([jnp.where(low, pair, zero), jnp.where(low, zero, pair)], axis=0)

    def keys(k):
        return doubled(qkv[:, pl.ds(1024 + 128 * (k // 2), 128)], k % 2, low)

    def values(k):
        return doubled(qkv[:, pl.ds(1536 + 128 * (k // 2), 128)], k % 2, low)

    for first in (0, 4):
        some = range(first, first + 4)
        scores = [mm_nt(heads(qkv, k), keys(k)) * 0.125 for k in some]
        scores = [jnp.where(allowed2, score, -1000000000.0) for score in scores]
        peaks = [jnp.max(score, axis=1, keepdims=True) for score in scores]
        raised = [jnp.exp(score - peak) for score, peak in zip(scores, peaks)]
        scales = [1.0 / jnp.sum(value, axis=1, keepdims=True) for value in raised]
        prob = [value * scale for value, scale in zip(raised, scales)]
        both = [mm(value.astype(BF16), values(k)) for value, k in zip(prob, some)]
        for k, value, pair in zip(some, prob, both):
            probs[k] = value
            attn[:, pl.ds(128 * k, 128)] = jnp.where(low, pair[:TOK], pair[TOK:]).astype(BF16)
        if first == 0:
            outputs.run()
        else:
            experts.step()
    a1t[...] = a1_ref[...].T
    outputs.settle()

    for j in range(4):
        part_j = pl.ds(256 * j, 256)
        h_ref[:, part_j] = x_ref[:, part_j].astype(F32) + mm(
            attn[...], cols_a(OUTPUTS[j // 2], 256 * (j % 2), 256)
        )
    h = h_ref[...]
    r2 = lax.rsqrt(jnp.mean(h * h, axis=1, keepdims=True) + EPS)
    a2 = (h * r2 * gain2).astype(BF16)
    a2_all[own, pl.ds(0, D)] = a2
    logits = jnp.where(lane < EXPERTS, mm(a2, misc), -jnp.inf)
    lexp = jnp.exp(logits - jnp.max(logits, axis=1, keepdims=True))
    rprobs = lexp / jnp.sum(lexp, axis=1, keepdims=True)
    gates = jnp.where(named, rprobs, 0.0)
    top, rest_of = split_two(gates)
    a2_all[own, pl.ds(D, 128)] = (top.astype(F32) + pltpu.roll(rest_of.astype(F32), EXPERTS, 1)).astype(BF16)
    a2_copies = swap(a2_all, a2_all, 0, TOK)
    experts.run()
    sibling = shifted(at, "c", 0)
    beside, across = pl.ds(TOK, TOK), pl.ds(3 * TOK, TOK)
    a2_own = pairs.push(a2_all.at[own], a2_all.at[pl.ds(2 * TOK, TOK)], sibling)
    arrived(g_copies)
    g_on = pairs.push(g_all.at[beside], g_all.at[across], sibling)
    arrived([g_own, g_on])
    gt[...] = g_all[...].T
    attnt[...] = attn[...].T
    experts.settle()
    links.turn()
    arrived(a2_copies)
    a2_on = pairs.push(a2_all.at[beside], a2_all.at[across], sibling)
    arrived([a2_own, a2_on])

    dgates = jnp.zeros((4 * TOK, 128), F32)
    for el in range(2):
        e = 2 * at["x"] + el
        extra = a2_all[:, pl.ds(D, 128)].astype(F32)
        gate_e = jnp.sum(jnp.where((lane == e) | (lane == e + EXPERTS), extra, 0.0), axis=1, keepdims=True)
        v = mm(a2_all[:, pl.ds(0, D)], cols_w(el, 0, 256))
        up = mm(a2_all[:, pl.ds(0, D)], cols_w(el, 256, 256))
        back = mm(g_all[...], cols_w(el, 512, 256))
        s = 1.0 / (1.0 + jnp.exp(-v))
        silu = v * s
        hidden = (silu * up).astype(BF16).astype(F32)
        dgates = dgates + jnp.where(lane == e, jnp.sum(hidden * back, axis=1, keepdims=True), 0.0)
        back = back * gate_e
        mid[el, :, pl.ds(0, 256)] = (back * up * s * (1.0 + v * (1.0 - s))).astype(BF16)
        mid[el, :, pl.ds(256, 256)] = (back * silu).astype(BF16)
        mid[el, :, pl.ds(512, 256)] = (hidden * gate_e).astype(BF16)
    dg_ref[...] = dgates

    def tile_w(el, t, lower, count):
        return cols_w(el, lower, count, ys=(t // 2,), zs=(2 * lax.rem(t, 2), 2 * lax.rem(t, 2) + 1))

    def da2_tile(t, carry):
        total = jnp.zeros((4 * TOK, 256), F32)
        for el in range(2):
            total = total + mm_nt(mid[el, :, pl.ds(0, 512)], tile_w(el, t, 0, 512))
        columns = pl.ds(pl.multiple_of(256 * t, 256), 256)
        da2_ref[:, columns] = total[: 2 * TOK]
        sib_d[:, columns] = total[2 * TOK :].astype(BF16)
        return carry

    def two_lanes(value):
        top, rest_of = split_two(value)
        return (top.astype(F32) + pltpu.roll(rest_of.astype(F32), EXPERTS, 1)).astype(BF16)

    def one_lane(extra):
        extra = extra.astype(F32)
        return extra + pltpu.roll(extra, 128 - EXPERTS, 1)

    lax.fori_loop(0, 4, da2_tile, 0)
    gates_at = pl.ds(D, 128)
    sib_d[:, gates_at] = two_lanes(dg_ref[pl.ds(2 * TOK, 2 * TOK), :])
    sib_copy = pairs.push(sib_d, from_d, sibling)
    a2t[...] = a2_all[:, pl.ds(0, D)].T
    sib_copy.wait_recv()
    ret_d[:, pl.ds(0, D)] = (da2_ref[beside, :] + from_d[beside, pl.ds(0, D)].astype(F32)).astype(BF16)
    ret_d[:, gates_at] = two_lanes(
        jnp.where(lane < EXPERTS, dg_ref[beside, :] + one_lane(from_d[beside, gates_at]), 0.0)
    )
    d_copies = swap_back(ret_d, got_d)

    for el in range(2):
        for j in range(3):
            left = a2t if j < 2 else gt
            put_w(el, 256 * j, mm(left[...], mid[el, :, pl.ds(256 * j, 256)]))
    links.turned()
    expert_sums = scatters(*EXPERT_SUMS)
    expert_sums.step()

    def y_tile(t, carry):
        total = jnp.zeros((4 * TOK, 256), F32)
        for el in range(2):
            total = total + mm_nt(mid[el, :, pl.ds(512, 256)], tile_w(el, t, 512, 256))
        columns = pl.ds(pl.multiple_of(256 * t, 256), 256)
        y_ref[:, columns] = total[: 2 * TOK]
        sib_y[:, columns] = total[2 * TOK :].astype(BF16)
        return carry

    lax.fori_loop(0, 4, y_tile, 0)
    y_own = pairs.push(sib_y, from_y, sibling)

    arrived(d_copies)
    dgates = dg_ref[own, :] + one_lane(from_d[own, gates_at]) + one_lane(got_d[:, gates_at])
    dp = jnp.where(named, dgates, 0.0)
    dlogits = (rprobs * (dp - jnp.sum(rprobs * dp, axis=1, keepdims=True))).astype(BF16)
    da2 = da2_ref[own, :] + from_d[own, pl.ds(0, D)].astype(F32) + got_d[:, pl.ds(0, D)].astype(F32)
    da2 = da2 + mm_nt(dlogits, misc)
    h = h_ref[...]
    misc_grad = mm_tn(a2_all[own, pl.ds(0, D)], dlogits)
    gain_two = (da2 * h * r2).astype(BF16)
    scaled = gain2 * da2
    dh = g_ref[...].astype(F32) + r2 * scaled - h * (r2 * r2 * r2) * jnp.mean(scaled * h, axis=1, keepdims=True)
    branch = dh.astype(BF16)
    dh_ref[...] = dh
    for j in range(4):
        put_a(OUT_SUMS[j // 2], 256 * (j % 2), mm(attnt[...], branch[:, 256 * j : 256 * j + 256]))
    misc_grad = misc_grad + mm_tn(gain_two, jnp.where(u_index == 5, 1.0, 0.0).astype(BF16))
    put_a(OUT_SUMS[1], 512, misc_grad)
    out_sums = scatters(*OUT_SUMS)
    out_sums.step()
    for t in range(4):
        dattn = mm_nt(branch[:, :512], tile_a(OUTPUTS[0], t, 512)) + mm_nt(branch[:, 512:], tile_a(OUTPUTS[1], t, 512))
        dattn_ref[:, pl.ds(256 * t, 256)] = dattn.astype(BF16)

    y_own.wait_recv()
    ret_y[...] = (y_ref[beside, :] + from_y[beside, :].astype(F32)).astype(BF16)
    y_copies = swap_back(ret_y, got_y)
    for first in (0, 4):
        some = range(first, first + 4)
        stacks = [heads(dattn_ref, k) for k in some]
        dprob = [mm_nt(stack, values(k)) for stack, k in zip(stacks, some)]
        parts = [probs[k] * value for k, value in zip(some, dprob)]
        sums_of = [jnp.sum(value, axis=1, keepdims=True) for value in parts]
        ds = [(value - probs[k] * total).astype(BF16) for k, value, total in zip(some, parts, sums_of)]
        dq = [mm(value, keys(k)) * 0.125 for value, k in zip(ds, some)]
        dk = [mm_tn(value, heads(qkv, k)) * 0.125 for value, k in zip(ds, some)]
        dv = [mm_tn(probs[k].astype(BF16), stack) for k, stack in zip(some, stacks)]
        dk = [value + pltpu.roll(value, 64, 1) for value in dk]
        dv = [value + pltpu.roll(value, 64, 1) for value in dv]
        for k, value in zip(some, dq):
            value = jnp.where(low, value[:TOK], value[TOK:])
            dqkv[:, pl.ds(128 * k, 128)] = turn(value, cosine, -sine).astype(BF16)
        for i in (0, 2):
            column = 64 * (first + i)
            value = turn(jnp.where(low, dk[i], dk[i + 1]), cosine, -sine)
            dqkv[:, pl.ds(1024 + column, 128)] = value.astype(BF16)
            dqkv[:, pl.ds(1536 + column, 128)] = jnp.where(low, dv[i], dv[i + 1]).astype(BF16)
        if first == 0:
            early = scatters(*EARLY)
            for j in range(4):
                put_a(j // 2, 256 * (j % 2), mm(a1t[...], dqkv[:, pl.ds(256 * TILES[j], 256)]))
            early.step()
            expert_sums.step()
            out_sums.step()
    late = [scatters(u) for u in LATE]
    for j in range(4, 8):
        put_a(j // 2, 256 * (j % 2), mm(a1t[...], dqkv[:, pl.ds(256 * TILES[j], 256)]))
        if j % 2:
            late[j // 2 - 2].step()
    early.step()
    out_sums.step()
    expert_sums.step()
    for t in range(4):
        total = jnp.zeros((TOK, 256), F32)
        for j in range(8):
            left = dqkv[:, pl.ds(256 * TILES[j], 256)]
            total = total + mm_nt(left, tile_a(j // 4, t, 256, 256 * (j % 4)))
        da1_ref[:, pl.ds(256 * t, 256)] = total
    da1 = da1_ref[...]
    x = x_ref[...].astype(F32)
    for group in late:
        group.step()
    scaled = gain1 * da1
    dx_ref[...] = (
        dh_ref[...] + r1 * scaled - x * (r1 * r1 * r1) * jnp.mean(scaled * x, axis=1, keepdims=True)
    )
    for group in late:
        group.step()
    early.step()
    out_sums.step()
    arrived(y_copies)
    out_ref[...] = (
        h_ref[...] + y_ref[own, :] + from_y[own, :].astype(F32) + got_y[...].astype(F32)
    ).astype(BF16)
    groups = late + [early, out_sums, expert_sums]
    while any(group.live for group in groups):
        for group in groups:
            group.step()
    product = jnp.zeros((ROWS_A, 1), F32)
    for slot, tile in enumerate(TILES):
        block = sum_all[:, pl.ds(256 * slot, 256)]
        sum_in[:, pl.ds(256 * tile, 256)] = block
        product = product + jnp.sum(block * in_ref[:, pl.ds(256 * tile, 256)].astype(F32), axis=1, keepdims=True)
    sum_out[...] = sum_more[:, pl.ds(0, D)]
    own_gain = jnp.sum(jnp.where(lane == 4, src_in[:, pl.ds(MISC, 128)].astype(F32), 0.0), axis=1, keepdims=True)
    tail = jnp.where(lane == 4, product / own_gain, sum_more[:, pl.ds(D, 128)])
    tail = jnp.concatenate([tail, jnp.zeros((128 - ROWS_A, 128), F32)], axis=0)
    small_ref[...] = tail.T[:8, :ROWS_A]
    links.close()
    pairs.close()


SEMS = 90
PAIR_SEMS = 14
VMEM_LIMIT = 60 * 1024 * 1024


def whole(tokens, cotangent, seg, routes, attn_in, attn_out, gain_attn, gain_ffn, router, expert_weight):
    buffers = [pltpu.VMEM(unit_shape(unit), BF16) for unit in GATHERS + SUMS]
    buffers += [pltpu.VMEM(shape, BF16) for u in SUM_ORDER for shape in Scatter.shapes(SUMS[u])]
    vmem = pl.BlockSpec(memory_space=pltpu.VMEM)
    return pl.pallas_call(
        whole_body,
        out_shape=(
            jax.ShapeDtypeStruct((TOK, D), BF16),
            jax.ShapeDtypeStruct((TOK, D), F32),
            jax.ShapeDtypeStruct((ROWS_A, 2048), F32),
            jax.ShapeDtypeStruct((ROWS_A, D), F32),
            jax.ShapeDtypeStruct((8, ROWS_A), F32),
            jax.ShapeDtypeStruct((ROWS_W, COLS_W), F32),
        ),
        in_specs=[vmem] * 10,
        out_specs=(vmem,) * 6,
        scratch_shapes=list(LAYER_SCRATCH)
        + buffers
        + [pltpu.SemaphoreType.DMA((SEMS,)), pltpu.SemaphoreType.DMA((SEMS,)), pltpu.SemaphoreType.REGULAR]
        + [pltpu.SemaphoreType.DMA((PAIR_SEMS,))] * 2,
        compiler_params=pltpu.CompilerParams(
            collective_id=0, has_side_effects=True, vmem_limit_bytes=VMEM_LIMIT
        ),
    )(tokens, cotangent, seg, routes, attn_in, attn_out, gain_attn, gain_ffn, router, expert_weight)


def emit_body(*refs):
    big, small, outs = refs[:5], refs[5], refs[6:]
    for source, target in zip(big, outs):
        target[...] = source[...]
    router, gain1, gain2 = outs[5:]
    router[...] = small[0:4, :]
    gain1[...] = small[4:5, :]
    gain2[...] = small[5:6, :]


def emit(big, small):
    vmem = pl.BlockSpec(memory_space=pltpu.VMEM)
    shapes = [jax.ShapeDtypeStruct(value.shape, value.dtype) for value in big]
    shapes += [jax.ShapeDtypeStruct((rows, ROWS_A), F32) for rows in (EXPERTS, 1, 1)]
    return pl.pallas_call(
        emit_body, out_shape=tuple(shapes), in_specs=[vmem] * 6, out_specs=(vmem,) * 8
    )(*big, small)


def local(
    tokens, segment_ids, routes, gain_attn, attn_in, attn_out, gain_ffn, router, expert_weight, cotangent
):
    output, grad, sum_in, sum_out, small, sum_w = whole(
        tokens, cotangent, segment_ids, routes.T, attn_in, attn_out,
        gain_attn[None, :], gain_ffn[None, :], router.T, expert_weight,
    )
    output, grad, sum_in, sum_out, sum_w, router_grad, gain1, gain2 = emit(
        (output, grad, sum_in, sum_out, sum_w), small
    )
    return (output, grad, gain1[0], sum_in, sum_out, gain2[0], router_grad.T, sum_w)


def solution(mesh):
    return jax.shard_map(
        local,
        mesh=mesh,
        in_specs=(
            P(("fsdp", "rep"), None),
            P(("fsdp", "rep"), None),
            P(("fsdp", "rep"), None),
            P("fsdp"),
            P("fsdp", None),
            P("fsdp", None),
            P("fsdp"),
            P("fsdp", None),
            P("fsdp", None),
            P(("fsdp", "rep"), None),
        ),
        out_specs=(
            P(("fsdp", "rep"), None),
            P(("fsdp", "rep"), None),
            P("fsdp"),
            P("fsdp", None),
            P("fsdp", None),
            P("fsdp"),
            P("fsdp", None),
            P("fsdp", None),
        ),
        check_vma=False,
    )
```

time: 2010 us -> 114 us (0.06)
  waiting for transfers between devices: 1180 us -> 0 us
  blocking collectives: 592 us -> 0 us
  Pallas kernels: 0 us -> 113 us
  matrix products: 97.5 us -> 0 us
  local copies, waits for them, and re-layouts: 56.6 us -> 0 us
  other arithmetic: 46.4 us -> 0 us
    reduce_scatter x3 -> x0, waiting for transfers between devices: 853 us -> none  [the longest x2 529 us: local(): lax.psum_scatter(totals, 'fsdp', scatter_dimension=0, tiled=True)]
    unnamed x3 -> x0, blocking collectives: 428 us -> none
    all_gather x6 -> x0, waiting for transfers between devices: 172 us -> none  [the longest x2 172 us: collect(): experts = lax.all_gather(expert_weight, 'fsdp', axis=0, tiled=True)]
    all_gather x2 -> x0, blocking collectives: 153 us -> none  [collect(): lax.all_gather(router, 'fsdp', axis=0, tiled=True)]
    unnamed x12 -> x0, waiting for transfers between devices: 142 us -> none
    pallas_call x0 -> x2, Pallas kernels: none -> 113 us  [the longest x1 110 us: whole(): pl.pallas_call(whole_body, out_shape=(jax.ShapeDtypeStruct((TOK, D), BF16...]
    dot_general x44 -> x0, matrix products: 97.5 us -> none  [the longest x2 12.6 us: micro_backward(): jnp.einsum('td,tw->dw', a1, d_qkv, preferred_element_type=jnp.float32)]
    concatenate x2 -> x0, local copies, waits for them, and re-layouts: 24.8 us -> none  [the longest x1 24.7 us: local(): jnp.concatenate([part_one, part_two], axis=-1)]
  transfers between devices with their start and end apart: 11 -> 0, of which waited for: 7 -> 0; matrix products, arithmetic and copies ran while one was open for 5% -> 0% of each run, Pallas kernels for 0% -> 0%
where the time goes in v1:
time: 114 us
  Pallas kernels  113 us (99%)
    pallas_call x1, Pallas kernels, whole(): pl.pallas_call(whole_body, out_shape=(jax.ShapeDtypeStruct((TOK, D), BF16...  110 us
    pallas_call x1, Pallas kernels, emit(): pl.pallas_call(emit_body, out_shape=tuple(shapes), in_specs=[vmem] * 6, o...  2.41 us

profile of v1, /device:TPU:2, one launch (start us, length us, event | category | flops | bytes accessed | tf_op | source)
XLA Modules:
  0.0 113.6 jit_solution(3864788889918952938)
XLA Ops:
  0.6 110.5 %shard_map.161 = (bf16[128,1024]{1,0:T(8,128)(2,1)}, f32[128,1024]{1,0:T(8,128)}, f32[16,2048]{1,0:T(8,128)}, f32[16,1024]{1,0:T(8,128)}, f32[8,16]{1,0:T(8,128)}, /*index=5*/f32[64,1536]{1,0:T(8,128)}) custom-call(bf16[128,1024]{1,0:T(8,128)(2,1)} %x_ref.1, bf16[128,1024]{1,0:T(8,128)(2,1)} %g_ref.1, s32[2,64]{1,0:T(2,128)} %seg_ref.1, s32[2,128]{1,0:T(2,128)} %bitcast.7, ...), custom_call_target="tpu_custom_call" | custom-call | tf_op jit(solution)/shard_map/pallas_call | solution.py:891
  111.1 2.4 %shard_map.162 = (bf16[128,1024]{1,0:T(8,128)(2,1)}, f32[128,1024]{1,0:T(8,128)}, f32[16,2048]{1,0:T(8,128)}, f32[16,1024]{1,0:T(8,128)}, f32[64,1536]{1,0:T(8,1...) custom-call(bf16[128,1024]{1,0:T(8,128)(2,1)} %get-tuple-element.22.refs_0_, ...), custom_call_target="tpu_custom_call" | custom-call | tf_op jit(solution)/shard_map/pallas_call | solution.py:927

commit v2 on v1

--- a/solution.py
+++ b/solution.py
@@ -208,20 +208,20 @@
         else:
             mine = self.source_of(have)
             local = self.links.local(mine, have.of(self.dst, self.core))
-        plane = order[:2] if order[0] == "x" else order[:1]
-        ring = plane[-1]
-        direct = [self.push(mine, have, shifted(at, ring, step)) for step in (1, -1, 2)]
-        if "x" in plane:
-            halves = have.halves(self.rows, self.count)
-            for step in (0, 1, -1, 2):
-                for half, side in zip(halves, (1, -1)):
-                    target = shifted(shifted(at, "x", side), ring, step)
-                    direct.append(self.push(self.source_of(half), half, target))
-        yield
-        if self.core is not None:
+        plane = order[: 2 if order[0] == "x" else 1] if self.core is not None else ""
+        if plane:
+            ring = plane[-1]
+            direct = [self.push(mine, have, shifted(at, ring, step)) for step in (1, -1, 2)]
+            if "x" in plane:
+                halves = have.halves(self.rows, self.count)
+                for step in (0, 1, -1, 2):
+                    for half, side in zip(halves, (1, -1)):
+                        target = shifted(shifted(at, "x", side), ring, step)
+                        direct.append(self.push(self.source_of(half), half, target))
+            yield
             local.wait()
-        for copy in direct:
-            copy.wait_recv()
+            for copy in direct:
+                copy.wait_recv()
         for axis in plane:
             have = have.full(axis)
         for axis in order[len(plane) :]:
@@ -324,7 +324,12 @@
         piece = piece.moved(rest[0], 0)
         shapes += [half.shape(rows, count) for half in piece.halves(rows, count)]
         shapes += [piece.shape(rows, count)] * 2
-        shapes += [piece.moved(rest[1], 0).shape(rows, count)] * 3
+        piece = piece.moved(rest[1], 0)
+        if unit[0] < 2:
+            shapes += [piece.shape(rows, count)] * 3
+        else:
+            shapes += [half.shape(rows, count) for half in piece.halves(rows, count)]
+            shapes += [piece.shape(rows, count)] * 2
         return shapes + [(rows, count)] * (3 if order[0] == "x" else 1)
 
     def push(self, piece, core, target):
@@ -351,29 +356,31 @@
                 copy.wait_recv()
                 add_blocks(self.grad, half, core, [buffer])
             rest.pop(0)
-        last, ring = rest[:2]
-        theirs = piece.moved(last, shifted(at, last, 2)[last]).halves(rows, count)
-        far = [self.push(half, core, shifted(at, last, step)) for half, step in zip(theirs, (1, -1))]
-        yield
-        near = []
-        for index, step in enumerate((1, -1)):
-            theirs = piece.moved(last, shifted(at, last, step)[last])
-            copy, buffer = far[index]
-            copy.wait_recv()
-            add_blocks(self.grad, theirs.halves(rows, count)[index], core, [buffer])
-            near.append(self.push(theirs, core, shifted(at, last, step)))
-        yield
-        piece = piece.moved(last, at[last])
-        for copy, buffer in near:
-            copy.wait_recv()
-        add_blocks(self.grad, piece, core, [buffer for copy, buffer in near])
-        moves = [shifted(at, ring, step) for step in (1, -1, 2)]
-        direct = [self.push(piece.moved(ring, to[ring]), core, to) for to in moves]
-        yield
-        piece = piece.moved(ring, at[ring])
-        for copy, buffer in direct:
-            copy.wait_recv()
-        add_blocks(self.grad, piece, core, [buffer for copy, buffer in direct])
+        for axis in rest[: 1 if core is not None else 2]:
+            theirs = piece.moved(axis, shifted(at, axis, 2)[axis]).halves(rows, count)
+            far = [self.push(half, core, shifted(at, axis, step)) for half, step in zip(theirs, (1, -1))]
+            yield
+            near = []
+            for index, step in enumerate((1, -1)):
+                theirs = piece.moved(axis, shifted(at, axis, step)[axis])
+                copy, buffer = far[index]
+                copy.wait_recv()
+                add_blocks(self.grad, theirs.halves(rows, count)[index], core, [buffer])
+                near.append(self.push(theirs, core, shifted(at, axis, step)))
+            yield
+            piece = piece.moved(axis, at[axis])
+            for copy, buffer in near:
+                copy.wait_recv()
+            add_blocks(self.grad, piece, core, [buffer for copy, buffer in near])
+        if core is not None:
+            ring = rest[1]
+            moves = [shifted(at, ring, step) for step in (1, -1, 2)]
+            direct = [self.push(piece.moved(ring, to[ring]), core, to) for to in moves]
+            yield
+            piece = piece.moved(ring, at[ring])
+            for copy, buffer in direct:
+                copy.wait_recv()
+            add_blocks(self.grad, piece, core, [buffer for copy, buffer in direct])
         if self.order[0] == "x":
             other = piece.moved("x", 1 - at["x"])
             piece = piece.moved("x", at["x"])
@@ -617,6 +624,7 @@
     named = (route0 == lane) | (route1 == lane)
     inputs.step()
     outputs.step()
+    experts.step()
     power = lax.rem(lane, 32).astype(F32) * (2.0 / 64)
     angle = pos * jnp.exp(power * (-9.210340371976184))
     cosine = jnp.cos(angle)
@@ -857,6 +865,7 @@
         group.step()
     early.step()
     out_sums.step()
+    expert_sums.step()
     arrived(y_copies)
     out_ref[...] = (
         h_ref[...] + y_ref[own, :] + from_y[own, :].astype(F32) + got_y[...].astype(F32)
@@ -879,7 +888,7 @@
     pairs.close()
 
 
-SEMS = 90
+SEMS = 92
 PAIR_SEMS = 14
 VMEM_LIMIT = 60 * 1024 * 1024
 

time: 114 us -> 114 us (level)
  no operation moved by 1% of the time
where the time goes in v2:
time: 114 us
  Pallas kernels  113 us (99%)
    pallas_call x1, Pallas kernels, whole(): pl.pallas_call(whole_body, out_shape=(jax.ShapeDtypeStruct((TOK, D), BF16...  111 us
    pallas_call x1, Pallas kernels, emit(): pl.pallas_call(emit_body, out_shape=tuple(shapes), in_specs=[vmem] * 6, o...  2.41 us

profile of v2, /device:TPU:2, one launch (start us, length us, event | category | flops | bytes accessed | tf_op | source)
XLA Modules:
  0.0 114.1 jit_solution(1442930251998371562)
XLA Ops:
  0.6 111.0 %shard_map.161 = (bf16[128,1024]{1,0:T(8,128)(2,1)}, f32[128,1024]{1,0:T(8,128)}, f32[16,2048]{1,0:T(8,128)}, f32[16,1024]{1,0:T(8,128)}, f32[8,16]{1,0:T(8,128)}, /*index=5*/f32[64,1536]{1,0:T(8,128)}) custom-call(bf16[128,1024]{1,0:T(8,128)(2,1)} %x_ref.1, bf16[128,1024]{1,0:T(8,128)(2,1)} %g_ref.1, s32[2,64]{1,0:T(2,128)} %seg_ref.1, s32[2,128]{1,0:T(2,128)} %bitcast.7, ...), custom_call_target="tpu_custom_call" | custom-call | tf_op jit(solution)/shard_map/pallas_call | solution.py:900
  111.7 2.4 %shard_map.162 = (bf16[128,1024]{1,0:T(8,128)(2,1)}, f32[128,1024]{1,0:T(8,128)}, f32[16,2048]{1,0:T(8,128)}, f32[16,1024]{1,0:T(8,128)}, f32[64,1536]{1,0:T(8,1...) custom-call(bf16[128,1024]{1,0:T(8,128)(2,1)} %get-tuple-element.22.refs_0_, ...), custom_call_target="tpu_custom_call" | custom-call | tf_op jit(solution)/shard_map/pallas_call | solution.py:936
